TPU v7x, 32 devices: a whole 2x2x4 slice. The times are simulated.
32 devices in a mesh: groups: 2 (over x), ctx: 2 (over core), fsdp: 8 (over z, y).
Axes of the slice: x: 2, y: 2, z: 4, core: 2. Of those that a mesh axis runs over, the one named last changes fastest.
Arguments:
- hidden_in: bfloat16 [8192, 2048], P(('groups', 'ctx', 'fsdp')), parts along dimension 0, may hold values from -6 to 6
- qkv_weight: bfloat16 [2048, 4096], P(None, 'fsdp'), may hold values from -0.125 to 0.125
- ab_weight: bfloat16 [2048, 32], replicated, may hold values from -0.125 to 0.125
- conv_weight: float32 [4, 4096], replicated, may hold values from -3 to 3
- decay_rate: float32 [16], replicated, may hold values from 7.324219e-05 to 0.3
- dt_bias: float32 [16], replicated, may hold values from -3 to -1
- norm_gain: float32 [128], replicated, may hold values from 0.1 to 1.9
- previous_tail: bfloat16 [6, 4096], P('groups'), parts along dimension 0, may hold values from -6 to 6
- window_entry_state: float32 [32, 128, 128], P('groups'), parts along dimension 0, may hold values from -3 to 3
Outputs:
- head_out: bfloat16 [8192, 2048], P(('groups', 'ctx', 'fsdp')), parts along dimension 0
There are 2 independent parts, one for each index of `groups`. A program takes and returns all parts, laid end to end along the dimension named above; an argument that names none is the same for every part. Nothing has to cross between parts.
All inputs are finite; a program needn't handle non-finite values.
Results may differ from a plain program's by a relative error of at most 0.0065.
Values may be sent and summed in bfloat16 or wider, within the bound.
A program may use at most 320 MiB of HBM per device.

v0:
```python
import jax
import jax.numpy as jnp
from jax import lax
from jax.sharding import PartitionSpec as P

HK = 8
HV = 16
DK = 128
DV = 128
SPAN = 64
exact_product = lax.Precision.HIGHEST


def shifted(array, axis, by):
    peers = lax.axis_size(axis)
    pairs = [(i, i + by) for i in range(peers) if 0 <= i + by < peers]
    return lax.ppermute(array, axis, pairs)


def entering(part, axis, combine, identity):
    place = lax.axis_index(axis)
    gathered = jax.tree.map(lambda a: lax.all_gather(a, axis), part)
    state = jax.tree.map(lambda a, e: jnp.zeros_like(a) + jnp.asarray(e, a.dtype), part, identity)

    def one(hop, state):
        return combine(
            state, jax.tree.map(lambda a: lax.dynamic_index_in_dim(a, hop, 0, False), gathered)
        )

    return lax.fori_loop(0, place, one, state)


def unit_norm(vectors):
    return vectors * lax.rsqrt(jnp.sum(vectors * vectors, axis=-1, keepdims=True) + 1e-06)


def convolve(before, mixed_qkv, conv_weight):
    length = mixed_qkv.shape[0]
    padded = jnp.concatenate([before, mixed_qkv], axis=0).astype(jnp.float32)
    summed = jnp.zeros((length, mixed_qkv.shape[1]), jnp.float32)
    for offset in range(conv_weight.shape[0]):
        summed = summed + conv_weight[offset] * padded[offset : offset + length]
    return jax.nn.silu(summed)


def to_spans(tensor, span_len):
    length, head_count = (tensor.shape[0], tensor.shape[1])
    shaped = tensor.reshape((length // span_len, span_len, head_count) + tensor.shape[2:])
    return jnp.moveaxis(shaped, 2, 1)


def head_inputs(conv_out, gate_logits, decay_rate, dt_bias):
    length = conv_out.shape[0]
    queries = unit_norm(conv_out[:, : HK * DK].reshape(length, HK, DK)) * DK ** (-0.5)
    head_keys = unit_norm(conv_out[:, HK * DK : 2 * HK * DK].reshape(length, HK, DK))
    values = conv_out[:, 2 * HK * DK :].reshape(length, HV, DV)
    queries = jnp.repeat(queries, HV // HK, axis=1)
    head_keys = jnp.repeat(head_keys, HV // HK, axis=1)
    write_rate = jax.nn.sigmoid(gate_logits[:, HV:])
    logdecay = -decay_rate * jax.nn.softplus(gate_logits[:, :HV] + dt_bias)
    return [to_spans(item, SPAN) for item in (queries, head_keys, values, write_rate, logdecay)]


def lower_inverse(strict_part):
    span_len = strict_part.shape[-1]
    unit_span = jnp.eye(span_len, dtype=strict_part.dtype)
    inverse = unit_span - strict_part
    power = strict_part
    reach = 2
    while reach < span_len:
        power = jnp.einsum("...ij,...jk->...ik", power, power, precision=exact_product)
        inverse = inverse + jnp.einsum(
            "...ij,...jk->...ik", inverse, power, precision=exact_product
        )
        reach = reach * 2
    return inverse


def span_terms(queries, head_keys, values, write_rate, logdecay):
    span_len = logdecay.shape[-1]
    cumulative = jnp.cumsum(logdecay, axis=-1)
    row_index = lax.broadcasted_iota(jnp.int32, (span_len, span_len), 0)
    col_index = lax.broadcasted_iota(jnp.int32, (span_len, span_len), 1)
    lower_mask = row_index >= col_index
    gap_log = cumulative[..., :, None] - cumulative[..., None, :]
    factor = jnp.where(lower_mask, jnp.exp(jnp.where(lower_mask, gap_log, 0.0)), 0.0)
    strict = jnp.where(row_index > col_index, factor, 0.0)
    key_products = jnp.einsum("...ik,...jk->...ij", head_keys, head_keys, precision=exact_product)
    query_products = jnp.einsum("...ik,...jk->...ij", queries, head_keys, precision=exact_product)
    inverse = lower_inverse(write_rate[..., :, None] * key_products * strict)
    growth = jnp.exp(cumulative)
    right_sides = jnp.concatenate(
        [write_rate[..., None] * values, (write_rate * growth)[..., None] * head_keys], axis=-1
    )
    solved = jnp.einsum("...ij,...jc->...ic", inverse, right_sides, precision=exact_product)
    new_values = solved[..., : values.shape[-1]]
    key_weights = solved[..., values.shape[-1] :]
    scores = query_products * factor
    window_local_output = jnp.einsum(
        "...ij,...jv->...iv", scores, new_values, precision=exact_product
    )
    effective_query = growth[..., None] * queries - jnp.einsum(
        "...ij,...jk->...ik", scores, key_weights, precision=exact_product
    )
    span_end = cumulative[..., -1]
    tail_decay = jnp.exp(span_end[..., None] - cumulative)
    decayed_keys = head_keys * tail_decay[..., None]
    unit_key = jnp.eye(head_keys.shape[-1], dtype=logdecay.dtype)
    state_mapping = jnp.exp(span_end)[..., None, None] * unit_key - jnp.einsum(
        "...ck,...cj->...kj", decayed_keys, key_weights, precision=exact_product
    )
    shifted_state = jnp.einsum(
        "...ck,...cv->...kv", decayed_keys, new_values, precision=exact_product
    )
    return (effective_query, window_local_output, state_mapping, shifted_state)


def finish(result_rows, norm_gain):
    mean_square = jnp.mean(result_rows * result_rows, axis=-1, keepdims=True)
    normed = result_rows * lax.rsqrt(mean_square + 1e-06) * norm_gain
    normed = jnp.moveaxis(normed, 1, 2)
    return normed.reshape(
        normed.shape[0] * normed.shape[1], normed.shape[2] * normed.shape[3]
    ).astype(jnp.bfloat16)


def compose(former_piece, latter_piece):
    joined_map = jnp.einsum(
        "hkj,hjm->hkm", latter_piece[0], former_piece[0], precision=exact_product
    )
    combined_state = (
        jnp.einsum("zom,zmg->zog", latter_piece[0], former_piece[1], precision=exact_product)
        + latter_piece[1]
    )
    return (joined_map, combined_state)


def shards(
    hidden_in,
    qkv_weight,
    ab_weight,
    conv_weight,
    decay_rate,
    dt_bias,
    norm_gain,
    previous_tail,
    window_entry_state,
):
    mixed_qkv = jnp.dot(
        hidden_in,
        lax.all_gather(qkv_weight, "fsdp", axis=1, tiled=True),
        preferred_element_type=jnp.float32,
    ).astype(jnp.bfloat16)
    gate_logits = jnp.dot(hidden_in, ab_weight, preferred_element_type=jnp.float32)
    tail_rows = previous_tail.shape[0]
    received = shifted(mixed_qkv[mixed_qkv.shape[0] - tail_rows :], ("ctx", "fsdp"), 1)
    before = jnp.where(lax.axis_index(("ctx", "fsdp")) == 0, previous_tail, received)
    conv_out = convolve(before, mixed_qkv, conv_weight)
    spanned = head_inputs(conv_out, gate_logits, decay_rate, dt_bias)
    effective_query, window_local_output, state_mapping, shifted_state = span_terms(*spanned)
    unit_maps = jnp.broadcast_to(jnp.eye(DK, dtype=jnp.float32), (HV, DK, DK))
    empty_state = jnp.zeros((HV, DK, DV), jnp.float32)

    def advance(carried, items):
        carry_map, carried_over_state = carried
        per_step_query, per_step_local, per_step_mapping, step_offset = items
        adjusted_result = jnp.einsum(
            "hck,hkj->hcj", per_step_query, carry_map, precision=exact_product
        )
        layer_result = per_step_local + jnp.einsum(
            "gpi,gib->gpb", per_step_query, carried_over_state, precision=exact_product
        )
        carry_map = jnp.einsum("hkj,hjm->hkm", per_step_mapping, carry_map, precision=exact_product)
        carried_over_state = (
            jnp.einsum(
                "zom,zmg->zog", per_step_mapping, carried_over_state, precision=exact_product
            )
            + step_offset
        )
        return ((carry_map, carried_over_state), (adjusted_result, layer_result))

    own_pair, (adjusted_result, incomplete_output) = lax.scan(
        advance,
        (unit_maps, empty_state),
        (effective_query, window_local_output, state_mapping, shifted_state),
    )
    identity = (unit_maps, empty_state)
    leading_pair = entering((own_pair[0], own_pair[1]), ("ctx", "fsdp"), compose, identity)
    opening_state = (
        jnp.einsum("zom,zmg->zog", leading_pair[0], window_entry_state, precision=exact_product)
        + leading_pair[1]
    )
    result_rows = incomplete_output + jnp.einsum(
        "elfx,lxw->elfw", adjusted_result, opening_state, precision=exact_product
    )
    return finish(result_rows, norm_gain)


def solution(mesh):
    placed = (
        P(("groups", "ctx", "fsdp"), None),
        P(None, "fsdp"),
        P(),
        P(),
        P(),
        P(),
        P(),
        P("groups", None),
        P("groups", None, None),
    )
    return jax.shard_map(
        shards,
        mesh=mesh,
        in_specs=placed,
        out_specs=P(("groups", "ctx", "fsdp"), None),
        check_vma=False,
    )
```

profile of v0, /device:TPU:31, one launch (start us, length us, event | category | flops | bytes accessed | tf_op | source)
XLA Modules:
  0.0 710.3 jit_solution(9324896033051884628)
XLA Ops:
  9.7 225.8 %all-gather.6.cloned.1.call-done = bf16[2048,4096]{1,0:T(8,128)(2,1)} async-done(((bf16[2048,512]{1,0:T(8,128)(2,1)}), bf16[2048,4096]{1,0:T(8,128)(2,1)}) %all-gather.6.cloned.1.call-update) | async-done | bytes 16777232 | tf_op jit(solution)/shard_map/all_gather | solution.py:151
  235.5 8.4 %convolution_convert_fusion = bf16[256,4096]{1,0:T(8,128)(2,1)S(1)} fusion(bf16[256,2048]{1,0:T(8,128)(2,1)S(1)} %copy-done, bf16[2048,4096]{1,0:T(8,128)(2,1)} %all-gather.6.cloned.1.call-done), kind=kOutput, calls=%fused_computation.35 | convolution fusion | flops 4296015872 | bytes 19922944 | tf_op jit(solution)/shard_map/dot_general | solution.py:149
  246.5 3.0 collective-permute-done
  250.9 2.8 divide_multiply_fusion
  257.3 3.5 fusion.45
  260.8 3.6 select_multiply_fusion
  266.6 2.7 fusion.88
  269.4 2.5 subtract_add_fusion
  278.7 2.5 fusion.90
  283.4 2.4 convolution_add_fusion.3
  289.3 4.5 fusion.34
  293.8 3.6 fusion.47
  297.4 3.9 fusion.40
  301.4 8.9 %fusion.46 = f32[4,16,128,128]{3,2,1,0:T(8,128)} fusion(f32[4,16,64,256]{3,2,1,0:T(8,128)S(1)} %fusion.34, f32[4,64,16,128]{3,1,0,2:T(8,128)S(1)} %bitcast.166, f32[4,16,64]{2,1,0:T(8,128)S(1)} %get-tuple-element.163), kind=kOutput, calls=%fused_computation.68 | convolution fusion | flops 805830656 | bytes 8421376 | tf_op jit(solution)/shard_map/...ck,...cv->...kv/dot_general | solution.py:112
  310.2 9.7 %multiply_subtract_fusion = f32[4,16,128,128]{3,2,1,0:T(8,128)} fusion(f32[128,128]{1,0:T(8,128)S(1)} %fusion.76, f32[4,16]{1,0:T(4,128)S(1)} %exp.36, f32[4,16,64,256]{3,2,1,0:T(8,128)S(1)} %fusion.34, f32[4,64,16,128]{3,1,0,2:T(8,128)S(1)} %bitcast.167, f32[4,16,64]{2,1,0:T(8,128)S(1)} %get-tuple-element.163), kind=kOutput, calls=%fused_computation.48 | convolution fusion | flops 807927808 | bytes 8488960 | tf_op jit(solution)/shard_map/...ck,...cj->...kj/dot_general | solution.py:109
  320.0 39.9 %while.30 = (s32[]{:T(128)}, f32[16,128,128]{2,1,0:T(8,128)S(1)}, f32[16,128,128]{2,1,0:T(8,128)S(1)}, f32[4,16,64,128]{3,2,0,1:T(8,128)}, f32[4,16,64,128]{3,2,...) while((s32[]{:T(128)}, f32[16,128,128]{2,1,0:T(8,128)S(1)}, ...), condition=%wide.region_4.5_spmd.clone, body=%wide.region_3.4_spmd.clone.sunk | while | flops 1208877056 | bytes 41423032 | solution.py:182
  324.7 2.9 fusion.157
  334.6 2.9 fusion.157
  344.6 2.9 fusion.157
  354.6 2.9 fusion.157
  361.7 126.7 %all-gather.8.cloned.1.call-done = f32[256,128,128]{2,1,0:T(8,128)} async-done(((f32[16,128,128]{2,1,0:T(8,128)}), f32[256,128,128]{2,1,0:T(8,128)}) %all-gather.8.cloned.1.call-update) | async-done | bytes 16777232 | tf_op jit(solution)/shard_map/all_gather | solution.py:22
  488.4 127.3 %all-gather.10.cloned.1.call-done = f32[256,128,128]{2,1,0:T(8,128)} async-done(((f32[16,128,128]{2,1,0:T(8,128)}), f32[256,128,128]{2,1,0:T(8,128)}) %all-gather.10.cloned.1.call-update) | async-done | bytes 16777232 | tf_op jit(solution)/shard_map/all_gather | solution.py:22
  615.9 80.2 %while.29 = (s32[]{:T(128)}, f32[16,128,128]{2,1,0:T(8,128)S(1)}, f32[16,128,128]{2,1,0:T(8,128)S(1)}, s32[]{:T(128)}, f32[16,16,128,128]{3,2,1,0:T(8,128)}, /*i...) while((s32[]{:T(128)}, f32[16,128,128]{2,1,0:T(8,128)S(1)}, ...), condition=%wide.region_6.7_spmd, body=%wide.region_5.6_spmd.sunk | while | flops 805568512 | bytes 11535499 | solution.py:30
  616.1 2.8 convolution_add_fusion.8
  618.9 2.4 fusion.146
  621.6 2.7 convolution_add_fusion.8
  624.3 2.4 fusion.146
  626.9 2.7 convolution_add_fusion.8
  632.2 2.7 convolution_add_fusion.8
  634.9 2.4 fusion.146
  637.5 2.7 convolution_add_fusion.8
  642.8 2.7 convolution_add_fusion.8
  645.5 2.4 fusion.146
  648.1 2.7 convolution_add_fusion.8
  653.5 2.7 convolution_add_fusion.8
  658.8 2.8 convolution_add_fusion.8
  661.6 2.4 fusion.146
  664.2 2.7 convolution_add_fusion.8
  669.5 2.7 convolution_add_fusion.8
  672.2 2.4 fusion.146
  674.9 2.7 convolution_add_fusion.8
  677.6 2.4 fusion.146
  680.2 2.7 convolution_add_fusion.8
  682.9 2.4 fusion.146
  685.5 2.7 convolution_add_fusion.8
  688.2 2.4 fusion.146
  690.8 2.7 convolution_add_fusion.8
  698.4 2.5 multiply_reduce_fusion
  (158 shorter events, 76.6 us)
Async XLA Ops:
  6.5 1.2 copy-start
  6.5 0.8 copy-start.15
  6.5 1.2 copy-start.9
  6.5 1.7 copy-start.13
  6.5 3.1 copy-start.10
  6.5 228.9 %all-gather.6.cloned.1.call-start = ((), (), s32[]{:S(2)}) async-start(), calls=%async_computation | async-start | bytes 18874368 | tf_op jit(solution)/shard_map/all_gather | solution.py:151
  7.3 481.1 %all-gather.8.cloned.1.call-start = ((), (), s32[]{:S(2)}) async-start(), calls=%async_computation.1 | async-start | bytes 17825792 | tf_op jit(solution)/shard_map/all_gather | solution.py:22
  9.7 239.8 %copy-start.11 = (bf16[3,4096]{1,0:T(4,128)(2,1)S(1)}, bf16[3,4096]{1,0:T(4,128)(2,1)}, u32[]{:S(2)}) copy-start(bf16[3,4096]{1,0:T(4,128)(2,1)} %param.20) | copy-start | bytes 73732
  244.5 5.0 collective-permute-start
  257.3 3.5 copy-start.12
  320.0 1.6 copy-start.5
  320.1 3.4 copy-start.2
  330.0 1.6 copy-start.5
  330.1 3.4 copy-start.2
  340.0 1.6 copy-start.5
  340.1 3.4 copy-start.2
  350.0 1.6 copy-start.5
  350.1 3.4 copy-start.2
  359.9 1.0 copy-start.3
  360.0 1.3 copy-start.4
  360.9 254.8 %all-gather.10.cloned.1.call-start = ((), (), s32[]{:S(2)}) async-start(), calls=%async_computation.2 | async-start | bytes 17825792 | tf_op jit(solution)/shard_map/all_gather | solution.py:22
  615.9 80.2 %copy-start.8 = (f32[16,128,128]{2,1,0:T(8,128)S(1)}, f32[16,128,128]{2,1,0:T(8,128)}, u32[]{:S(2)}) copy-start(f32[16,128,128]{2,1,0:T(8,128)} %param.21) | copy-start | bytes 3145732
  696.2 1.6 copy-start.6
  696.2 2.2 copy-start.7
  698.4 2.5 copy-start.14
  701.0 2.7 copy-start.1
Sparse Core Ops, SparseCore 0:
  9.4 226.0 all-gather.5
  361.1 127.2 all-gather.7
  490.6 125.0 all-gather.9
where the time goes:
time: 716 us; the launch traced here: 710 us
  waiting for transfers between devices  484 us (68%)
  matrix products  184 us (26%)
  local copies, waits for them, and re-layouts  16.5 us (2%)
  between operations  13.8 us (2%)
  other arithmetic  9.23 us (1%)
    all_gather x2, waiting for transfers between devices, entering(): gathered = jax.tree.map(lambda a: lax.all_gather(a, axis), part)  254 us
    all_gather x1, waiting for transfers between devices, shards(): lax.all_gather(qkv_weight, 'fsdp', axis=1, tiled=True)  226 us
    dot_general x15, matrix products, compose(): jnp.einsum('zom,zmg->zog', latter_piece[0], former_piece[1], precision=ex...  40.7 us
    dot_general x15, matrix products, compose(): jnp.einsum('hkj,hjm->hkm', latter_piece[0], former_piece[0], precision=ex...  36.3 us
  transfers between devices with their start and end apart: 4, of which 4 were waited for; matrix products, arithmetic and copies ran while one was open for 0% of the time, Pallas kernels for 0%

commit v1 on v0

--- a/solution.py
+++ b/solution.py
@@ -9,6 +9,18 @@
 DV = 128
 SPAN = 64
 exact_product = lax.Precision.HIGHEST
+
+
+def doubled_up(x, axis, dim):
+    ways, here, turn = (lax.axis_size(axis), lax.axis_index(axis), x.shape[dim])
+    line, have = (x, 1)
+    while have < ways:
+        line = jnp.concatenate(
+            [line, lax.ppermute(line, axis, [(d, (d - have) % ways) for d in range(ways)])],
+            axis=dim,
+        )
+        have = 2 * have
+    return jnp.roll(line, here * turn, axis=dim)
 
 
 def shifted(array, axis, by):
@@ -147,9 +159,7 @@
     window_entry_state,
 ):
     mixed_qkv = jnp.dot(
-        hidden_in,
-        lax.all_gather(qkv_weight, "fsdp", axis=1, tiled=True),
-        preferred_element_type=jnp.float32,
+        hidden_in, doubled_up(qkv_weight, "fsdp", 1), preferred_element_type=jnp.float32
     ).astype(jnp.bfloat16)
     gate_logits = jnp.dot(hidden_in, ab_weight, preferred_element_type=jnp.float32)
     tail_rows = previous_tail.shape[0]

time: 716 us -> 1020 us (1.42)
  waiting for transfers between devices: 484 us -> 750 us
  local copies, waits for them, and re-layouts: 16.5 us -> 41.2 us
    ppermute x0 -> x3, waiting for transfers between devices: none -> 493 us  [doubled_up(): lax.ppermute(line, axis, [(d, (d - have) % ways) for d in range(ways)])]
    all_gather x1 -> x0, waiting for transfers between devices: 226 us -> none  [shards(): lax.all_gather(qkv_weight, 'fsdp', axis=1, tiled=True)]
    unnamed x34 -> x51, local copies, waits for them, and re-layouts: 5.13 us -> 27.1 us
  transfers between devices with their start and end apart: 4 -> 6, of which waited for: 4 -> 6; matrix products, arithmetic and copies ran while one was open for 0% -> 1% of each run, Pallas kernels for 0% -> 0%
where the time goes in v1:
time: 1020 us
  waiting for transfers between devices  750 us (74%)
  matrix products  192 us (19%)
  local copies, waits for them, and re-layouts  41.2 us (4%)
  other arithmetic  16.9 us (2%)
  between operations  14.2 us (1%)
    ppermute x3, waiting for transfers between devices, doubled_up(): lax.ppermute(line, axis, [(d, (d - have) % ways) for d in range(ways)])  493 us
    all_gather x2, waiting for transfers between devices, entering(): gathered = jax.tree.map(lambda a: lax.all_gather(a, axis), part)  253 us
    dot_general x15, matrix products, compose(): jnp.einsum('zom,zmg->zog', latter_piece[0], former_piece[1], precision=ex...  41.3 us
    dot_general x15, matrix products, compose(): jnp.einsum('hkj,hjm->hkm', latter_piece[0], former_piece[0], precision=ex...  35.7 us
    unnamed x51, local copies, waits for them, and re-layouts  27.1 us
  transfers between devices with their start and end apart: 6, of which 6 were waited for; matrix products, arithmetic and copies ran while one was open for 1% of the time, Pallas kernels for 0%

profile of v1, /device:TPU:31, one launch (start us, length us, event | category | flops | bytes accessed | tf_op | source)
XLA Modules:
  0.0 1016.8 jit_solution(14191765541959267704)
XLA Ops:
  6.8 49.2 %collective-permute-done = bf16[2048,512]{1,0:T(8,128)(2,1)S(1)} collective-permute-done((bf16[2048,512]{1,0:T(8,128)(2,1)}, bf16[2048,512]{1,0:T(8,128)(2,1)S(1)}, u32[]{:S(2)}, u32[]{:S(2)}) %collective-permute-start) | collective-permute-done | bytes 2097184 | tf_op jit(solution)/shard_map/ppermute | solution.py:19
  56.0 3.0 pad_maximum_fusion.1
  59.1 92.3 %collective-permute-done.1 = bf16[2048,1024]{1,0:T(8,128)(2,1)S(1)} collective-permute-done((bf16[2048,1024]{1,0:T(8,128)(2,1)S(1)}, bf16[2048,1024]{1,0:T(8,128)(2,1)S(1)}, u32[]{:S(2)}, u32[]{:S(2)}) %collective-permute-start.1) | collective-permute-done | bytes 4194336 | tf_op jit(solution)/shard_map/ppermute | solution.py:19
  151.4 4.5 pad_maximum_fusion
  165.5 351.9 %collective-permute-done.2 = bf16[2048,2048]{1,0:T(8,128)(2,1)} collective-permute-done((bf16[2048,2048]{1,0:T(8,128)(2,1)}, bf16[2048,2048]{1,0:T(8,128)(2,1)}, u32[]{:S(2)}, u32[]{:S(2)}) %collective-permute-start.2) | collective-permute-done | bytes 8388640 | tf_op jit(solution)/shard_map/ppermute | solution.py:19
  517.4 8.3 constant_dynamic-update-slice_fusion.4
  525.7 3.2 constant_dynamic-update-slice_fusion.3
  532.7 8.4 constant_dynamic-update-slice_fusion
  541.1 8.4 fusion.36
  552.1 3.0 collective-permute-done.3
  556.5 3.0 divide_multiply_fusion
  562.7 3.5 fusion.53
  566.3 3.7 select_multiply_fusion
  574.7 2.6 subtract_add_fusion
  584.3 2.6 fusion.99
  595.6 4.7 fusion.42
  600.4 3.6 fusion.55
  604.0 3.9 fusion.48
  607.9 8.9 fusion.54
  616.8 9.4 multiply_subtract_fusion
  626.4 39.8 %while.30 = (s32[]{:T(128)}, f32[16,128,128]{2,1,0:T(8,128)S(1)}, f32[16,128,128]{2,1,0:T(8,128)S(1)}, f32[4,16,64,128]{3,2,0,1:T(8,128)}, f32[4,16,64,128]{3,2,...) while((s32[]{:T(128)}, f32[16,128,128]{2,1,0:T(8,128)S(1)}, ...), condition=%wide.region_4.5_spmd.clone, body=%wide.region_3.4_spmd.clone.sunk | while | flops 1208877056 | bytes 33033364 | solution.py:192
  626.5 3.3 fusion.165
  632.2 2.9 fusion.164
  636.4 3.3 fusion.165
  642.2 2.9 fusion.164
  646.4 3.3 fusion.165
  652.1 2.9 fusion.164
  656.3 3.2 fusion.165
  662.1 2.9 fusion.164
  667.9 125.7 %all-gather.5.cloned.1.call-done = f32[256,128,128]{2,1,0:T(8,128)} async-done(((f32[16,128,128]{2,1,0:T(8,128)}), f32[256,128,128]{2,1,0:T(8,128)}) %all-gather.5.cloned.1.call-update) | async-done | bytes 16777232 | tf_op jit(solution)/shard_map/all_gather | solution.py:34
  793.7 127.3 %all-gather.7.cloned.1.call-done = f32[256,128,128]{2,1,0:T(8,128)} async-done(((f32[16,128,128]{2,1,0:T(8,128)}), f32[256,128,128]{2,1,0:T(8,128)}) %all-gather.7.cloned.1.call-update) | async-done | bytes 16777232 | tf_op jit(solution)/shard_map/all_gather | solution.py:34
  921.2 80.2 %while.29 = (s32[]{:T(128)}, f32[16,128,128]{2,1,0:T(8,128)S(1)}, f32[16,128,128]{2,1,0:T(8,128)S(1)}, s32[]{:T(128)}, f32[16,16,128,128]{3,2,1,0:T(8,128)}, /*i...) while((s32[]{:T(128)}, f32[16,128,128]{2,1,0:T(8,128)S(1)}, ...), condition=%wide.region_6.7_spmd, body=%wide.region_5.6_spmd.sunk | while | flops 805568512 | bytes 11535491 | solution.py:42
  921.3 2.8 convolution_add_fusion.8
  926.7 2.7 convolution_add_fusion.8
  932.0 2.7 convolution_add_fusion.8
  937.3 2.7 convolution_add_fusion.8
  942.6 2.7 convolution_add_fusion.8
  947.9 2.7 convolution_add_fusion.8
  953.2 2.7 convolution_add_fusion.8
  958.6 2.8 convolution_add_fusion.8
  963.9 2.8 convolution_add_fusion.8
  969.3 2.7 convolution_add_fusion.8
  974.6 2.7 convolution_add_fusion.8
  979.9 2.7 convolution_add_fusion.8
  985.3 2.8 convolution_add_fusion.8
  990.6 2.7 convolution_add_fusion.8
  995.9 2.7 convolution_add_fusion.8
  1002.9 4.0 multiply_reduce_fusion
  (173 shorter events, 100.0 us)
Async XLA Ops:
  6.5 149.3 %copy-start = (bf16[256,2048]{1,0:T(8,128)(2,1)S(1)}, bf16[256,2048]{1,0:T(8,128)(2,1)}, u32[]{:S(2)}) copy-start(bf16[256,2048]{1,0:T(8,128)(2,1)} %param.13) | copy-start | bytes 3145732
  6.5 144.8 %copy-start.7 = (bf16[2048,512]{1,0:T(8,128)(2,1)S(1)}, bf16[2048,512]{1,0:T(8,128)(2,1)}, u32[]{:S(2)}) copy-start(bf16[2048,512]{1,0:T(8,128)(2,1)} %param.14) | copy-start | bytes 6291460
  6.5 787.1 %all-gather.5.cloned.1.call-start = ((), (), s32[]{:S(2)}) async-start(), calls=%async_computation | async-start | bytes 17825792 | tf_op jit(solution)/shard_map/all_gather | solution.py:34
  6.5 49.4 %collective-permute-start = (bf16[2048,512]{1,0:T(8,128)(2,1)}, bf16[2048,512]{1,0:T(8,128)(2,1)S(1)}, u32[]{:S(2)}, u32[]{:S(2)}) collective-permute-start(bf16[2048,512]{1,0:T(8,128)(2,1)} %param.14), channel_id=1, source_target_pairs={{0,7},{1,0},{2,1},{3,2},{4,3},{5,4},{6,5},{7,6},{8,15},{9,8},{10,9... | collective-permute-start | bytes 6291464 | tf_op jit(solution)/shard_map/ppermute | solution.py:19
  55.9 95.4 %copy-start.8 = (bf16[2048,512]{1,0:T(8,128)(2,1)}, bf16[2048,512]{1,0:T(8,128)(2,1)S(1)}, u32[]{:S(2)}) copy-start(bf16[2048,512]{1,0:T(8,128)(2,1)S(1)} %collective-permute-done) | copy-start | bytes 6291460
  58.9 96.9 %copy-start.19 = (f32[16]{0:T(128)S(1)}, f32[16]{0:T(128)}, u32[]{:S(2)}) copy-start(f32[16]{0:T(128)} %param.17) | copy-start | bytes 196
  59.0 96.9 %copy-start.13 = (bf16[2048,32]{0,1:T(8,128)(2,1)S(1)}, bf16[2048,32]{0,1:T(8,128)(2,1)}, u32[]{:S(2)}) copy-start(bf16[2048,32]{0,1:T(8,128)(2,1)} %param.15) | copy-start | bytes 393220
  59.0 97.3 %copy-start.17 = (f32[16]{0:T(128)S(1)}, f32[16]{0:T(128)}, u32[]{:S(2)}) copy-start(f32[16]{0:T(128)} %param.18) | copy-start | bytes 196
  59.0 92.4 %collective-permute-start.1 = (bf16[2048,1024]{1,0:T(8,128)(2,1)S(1)}, bf16[2048,1024]{1,0:T(8,128)(2,1)S(1)}, u32[]{:S(2)}, u32[]{:S(2)}) collective-permute-start(bf16[2048,1024]{1,0:T(8,128)(2,1)S(1)} %pad_maximum_fusion.1), channel_id=1, source_target_pairs={{0,6},{1,7},{2,0},{3,1},{4,2},{5,3},{6,4},{7,5},{8,14},{9,15},{10,... | collective-permute-start | bytes 12582920 | tf_op jit(solution)/shard_map/ppermute | solution.py:19
  151.4 4.5 copy-start.5
  155.8 361.6 %collective-permute-start.2 = (bf16[2048,2048]{1,0:T(8,128)(2,1)}, bf16[2048,2048]{1,0:T(8,128)(2,1)}, u32[]{:S(2)}, u32[]{:S(2)}) collective-permute-start(bf16[2048,2048]{1,0:T(8,128)(2,1)} %pad_maximum_fusion), channel_id=1, source_target_pairs={{0,4},{1,5},{2,6},{3,7},{4,0},{5,1},{6,2},{7,3},{8,12},{9,13},{10,... | collective-permute-start | bytes 25165832 | tf_op jit(solution)/shard_map/ppermute | solution.py:19
  157.8 1.5 copy-start.14
  157.8 2.4 copy-start.9
  160.2 2.9 copy-start.6
  525.7 3.2 copy-start.10
  541.1 14.0 %copy-start.15 = (bf16[3,4096]{1,0:T(4,128)(2,1)S(1)}, bf16[3,4096]{1,0:T(4,128)(2,1)}, u32[]{:S(2)}) copy-start(bf16[3,4096]{1,0:T(4,128)(2,1)} %param.20) | copy-start | bytes 73732
  550.2 5.0 collective-permute-start.3
  562.7 3.5 copy-start.16
  626.4 3.4 copy-start.2
  636.3 3.4 copy-start.2
  646.3 3.4 copy-start.2
  656.2 3.3 copy-start.2
  666.2 1.0 copy-start.3
  666.2 1.3 copy-start.4
  667.2 253.8 %all-gather.7.cloned.1.call-start = ((), (), s32[]{:S(2)}) async-start(), calls=%async_computation.1 | async-start | bytes 17825792 | tf_op jit(solution)/shard_map/all_gather | solution.py:34
  921.2 80.2 %copy-start.12 = (f32[16,128,128]{2,1,0:T(8,128)S(1)}, f32[16,128,128]{2,1,0:T(8,128)}, u32[]{:S(2)}) copy-start(f32[16,128,128]{2,1,0:T(8,128)} %param.21) | copy-start | bytes 3145732
  1001.3 1.6 copy-start.11
  1002.9 4.1 copy-start.18
  1007.0 2.7 copy-start.1
Sparse Core Ops, SparseCore 0:
  667.3 126.3 all-gather.4
  795.9 125.0 all-gather.6
